TPU v7x, 32 devices: a whole 2x2x4 slice. The times are simulated.
32 devices in a mesh: pool: 4 (over z), ctx: 8 (over y, x, core).
Axes of the slice: x: 2, y: 2, z: 4, core: 2. Of those that a mesh axis runs over, the one named last changes fastest.
Arguments:
- question_q: bfloat16 [2048, 4096], P('ctx', 'pool'), may hold values from -6 to 6
- question_kv: bfloat16 [2, 2048, 512], P(None, 'ctx', 'pool'), may hold values from -6 to 6
- cache_kv: bfloat16 [64, 2, 64, 512], P(('pool', 'ctx')), may hold values from -6 to 6
- placement: int32 [32], P('ctx'), may hold values from -1 to 63, as said below
- offsets: int32 [32], P('ctx'), may hold values from 0 to 1984
Outputs:
- attended: bfloat16 [2048, 4096], P('ctx', 'pool')
Inputs may be any that keep to these rules, and one draw needn't show every extreme that they name: `placement`: owner o's slots are entries o * 4 to o * 4 + 3; the live ones come first, every owner has at least one and some owner has all 4; no pool block is placed twice. Of the blocks held by the devices of one index c of ctx (ids b with (b // 2) % 8 == c), at most 4 are placed, and exactly 4 for some index.
All inputs are finite; a program needn't handle non-finite values.
Results may differ from a plain program's by a relative error of at most 0.012.
Values may be sent and summed in bfloat16 or wider, within the bound.
A program may use at most 64 MiB of HBM per device.

v0:
```python
import math

import jax
import jax.numpy as jnp
from jax import lax
from jax.sharding import PartitionSpec as P

HEAD_SIZE = 128


rope_base = 500000.0
masked_score = -1e30


def rope_tables(positions, half_width):
    frequency = rope_base ** (-jnp.arange(half_width, dtype=jnp.float32) / half_width)
    angles = positions.astype(jnp.float32)[:, None] * frequency[None, :]
    return (jnp.cos(angles), jnp.sin(angles))


def rotate(vectors, cosine, sine_part):
    half_width = vectors.shape[-1] // 2
    first_half = vectors[..., :half_width]
    second_half = vectors[..., half_width:]
    return jnp.concatenate(
        [
            first_half * cosine - second_half * sine_part,
            second_half * cosine + first_half * sine_part,
        ],
        axis=-1,
    )


def attend(carried, queries, key_rows, value_rows, allowed):
    running_max, totals, numerator = carried
    scores = jnp.einsum(
        "gqd,gkd->gqk", queries, key_rows, preferred_element_type=jnp.float32
    ) * HEAD_SIZE ** (-0.5)
    scores = jnp.where(allowed, scores, masked_score)
    new_max = jnp.maximum(running_max, jnp.max(scores, axis=2))
    weights = jnp.where(allowed, jnp.exp(scores - new_max[..., None]), 0.0)
    factor = jnp.exp(running_max - new_max)
    totals = totals * factor + jnp.sum(weights, axis=2)
    numerator = numerator * factor[..., None] + jnp.einsum(
        "gqk,gkd->gqd", weights.astype(jnp.bfloat16), value_rows, preferred_element_type=jnp.float32
    )
    return (new_max, totals, numerator)


def fold_blocks(carried, shard_piece, queries, block_offsets, block_live):
    piece_count = shard_piece.shape[0]
    block_len = shard_piece.shape[2]
    kv_width = shard_piece.shape[3]
    kv_heads = kv_width // HEAD_SIZE
    per_step = math.gcd(piece_count, max(1, 512 // block_len))
    step_count = piece_count // per_step
    offsets_here = block_offsets.reshape(step_count, per_step)
    live_here = block_live.reshape(step_count, per_step)
    parted = shard_piece.reshape(step_count, per_step, 2, block_len, kv_width)

    def fold_advance(state_now, scan_item):
        blocks_now, offset_now, live_now = scan_item
        key_rows = blocks_now[:, 0].reshape(per_step * block_len, kv_heads, HEAD_SIZE)
        cosine, sine_part = rope_tables(jnp.repeat(offset_now, block_len), HEAD_SIZE // 2)
        key_rows = rotate(
            key_rows.astype(jnp.float32), cosine[:, None, :], sine_part[:, None, :]
        ).astype(jnp.bfloat16)
        key_rows = key_rows.transpose(1, 0, 2)
        value_rows = (
            blocks_now[:, 1].reshape(per_step * block_len, kv_heads, HEAD_SIZE).transpose(1, 0, 2)
        )
        allowed = jnp.repeat(live_now, block_len)[None, None, :]
        return (attend(state_now, queries, key_rows, value_rows, allowed), None)

    carried, unused = lax.scan(fold_advance, carried, (parted, offsets_here, live_here))
    return carried


def shards(question_q, question_kv, cache_kv, placement, offsets):
    ctx_count = lax.axis_size("ctx")
    pool_count = lax.axis_size("pool")
    column = lax.axis_index("ctx")
    row_count = question_q.shape[0]
    kv_width = question_kv.shape[2]
    kv_heads = kv_width // HEAD_SIZE
    group_size = question_q.shape[1] // kv_width
    hold_count = cache_kv.shape[0]
    block_len = cache_kv.shape[2]
    all_ids, all_offsets = (
        lax.all_gather(placement, "ctx", axis=0, tiled=True),
        lax.all_gather(offsets, "ctx", axis=0, tiled=True),
    )
    slot_count = all_ids.shape[0]
    question_index = column * row_count + jnp.arange(row_count, dtype=jnp.int32)
    cos_query, sin_query = rope_tables(slot_count * block_len + question_index, HEAD_SIZE // 2)
    raw_queries = (
        question_q.reshape(row_count, kv_heads, group_size, HEAD_SIZE)
        .transpose(1, 2, 0, 3)
        .astype(jnp.float32)
    )
    queries = (
        rotate(raw_queries, cos_query, sin_query)
        .astype(jnp.bfloat16)
        .reshape(kv_heads, group_size * row_count, HEAD_SIZE)
    )
    raw_own = question_kv[0].reshape(row_count, kv_heads, HEAD_SIZE).astype(jnp.float32)
    own_keys = (
        rotate(raw_own, cos_query[:, None, :], sin_query[:, None, :])
        .astype(jnp.bfloat16)
        .reshape(row_count, kv_width)
    )
    own_pair = jnp.stack([own_keys, question_kv[1]], axis=0)
    query_rows = group_size * row_count
    carried = (
        jnp.full((kv_heads, query_rows), masked_score, jnp.float32),
        jnp.zeros((kv_heads, query_rows), jnp.float32),
        jnp.zeros((kv_heads, query_rows, HEAD_SIZE), jnp.float32),
    )
    local_blocks = lax.all_to_all(cache_kv, "pool", split_axis=3, concat_axis=0, tiled=True)
    local_count = pool_count * hold_count
    total_blocks = ctx_count * local_count
    gathered_index = jnp.arange(total_blocks, dtype=jnp.int32)
    source_column = gathered_index // local_count
    within = gathered_index % local_count
    block_ids = (
        within // hold_count * ctx_count + source_column
    ) * hold_count + within % hold_count
    matches = all_ids[None, :] == block_ids[:, None]
    block_live = jnp.any(matches, axis=1)
    block_offsets = jnp.sum(jnp.where(matches, all_offsets[None, :], 0), axis=1)
    carried = fold_blocks(
        carried,
        lax.all_gather(local_blocks, "ctx", axis=0, tiled=True),
        queries,
        block_offsets,
        block_live,
    )
    tiled_index = jnp.tile(question_index, group_size)
    shard_piece = lax.all_gather(own_pair, "ctx", axis=1, tiled=True)
    piece_rows = shard_piece.shape[1]
    step_len = math.gcd(piece_rows, 512)
    parted = shard_piece.reshape(2, piece_rows // step_len, step_len, kv_width).transpose(
        1, 0, 2, 3
    )

    def body_advance(state_now, scan_item):
        pair_now, sub_index = scan_item
        key_rows = pair_now[0].reshape(step_len, kv_heads, HEAD_SIZE).transpose(1, 0, 2)
        value_rows = pair_now[1].reshape(step_len, kv_heads, HEAD_SIZE).transpose(1, 0, 2)
        key_index = sub_index * step_len + jnp.arange(step_len, dtype=jnp.int32)
        allowed = (key_index[None, :] <= tiled_index[:, None])[None]
        return (attend(state_now, queries, key_rows, value_rows, allowed), None)

    result_state, unused = lax.scan(
        body_advance, carried, (parted, jnp.arange(piece_rows // step_len, dtype=jnp.int32))
    )
    carried = result_state
    running_max, totals, numerator = carried
    result = numerator / totals[..., None]
    result = (
        result.reshape(kv_heads, group_size, row_count, HEAD_SIZE)
        .transpose(2, 0, 1, 3)
        .reshape(row_count, kv_heads * group_size * HEAD_SIZE)
    )
    return result.astype(jnp.bfloat16)


def solution(mesh):
    in_specs = (
        P("ctx", "pool"),
        P(None, "ctx", "pool"),
        P(("pool", "ctx"), None, None, None),
        P("ctx"),
        P("ctx"),
    )
    out_specs = P("ctx", "pool")
    return jax.shard_map(shards, mesh=mesh, in_specs=in_specs, out_specs=out_specs, check_vma=False)
```

profile of v0, /device:TPU:0, one launch (start us, length us, event | category | flops | bytes accessed | tf_op | source)
XLA Modules:
  0.0 173.0 jit_solution(10024960865987775007)
XLA Ops:
  6.6 1.3 copy.18
  8.3 15.0 %all_to_all.18 = bf16[4,2,16384]{2,1,0:T(2,128)(2,1)S(1)} all-to-all(bf16[4,2,16384]{2,1,0:T(2,128)(2,1)S(1)} %reshape.542), channel_id=1, replica_groups=mesh['pool'=4,'ctx'=8] {'pool'}, dimensions={0} | all-to-all | bytes 524288 | tf_op jit(solution)/shard_map/all_to_all | solution.py:119
  23.7 1.0 copy.19
  29.3 8.0 %all-reduce.2 = (s32[32]{0:T(128)S(1)}, s32[32]{0:T(128)S(1)}) all-reduce(s32[32]{0:T(128)S(1)} %dynamic-update-slice, s32[32]{0:T(128)S(1)} %dynamic-update-slice.1), channel_id=1, replica_groups=mesh['pool'=4,'ctx'=8] {'ctx'}, use_global_device_ids=true, to_apply=%add | all-reduce | flops 64 | bytes 512
  39.0 12.9 %all-gather.3.cloned.1.call-done = bf16[64,2,64,128]{3,2,1,0:T(8,128)(2,1)} async-done(((bf16[8,2,64,128]{3,2,1,0:T(8,128)(2,1)}), bf16[64,2,64,128]{3,2,1,0:T(8,128)(2,1)}) %all-gather.3.cloned.1.call-update) | async-done | bytes 2097168 | tf_op jit(solution)/shard_map/all_gather | solution.py:133
  51.9 88.7 %while.31 = (s32[]{:T(128)}, f32[1,2048]{1,0:T(1,128)S(1)}, f32[1,2048]{1,0:T(1,128)S(1)}, f32[1,2048,128]{2,1,0:T(8,128)S(1)}, pred[8,8]{1,0:T(8,128)(4,1)S(1)}...) while((s32[]{:T(128)}, f32[1,2048]{1,0:T(1,128)S(1)}, ...), condition=%wide.region_5.6_spmd.clone, body=%wide.region_2.5_spmd.clone.sunk | while | flops 551921792 | bytes 34221840 | solution.py:75
  53.1 1.2 fusion.88
  54.5 2.8 %fusion.89 = (f32[2048]{0:T(1024)S(1)}, f32[512,2048]{1,0:T(8,128)}) fusion(pred[512]{0:T(512)(128)(4,1)S(1)} %broadcast_in_dim.139, bf16[1,2048,128]{2,1,0:T(8,128)(2,1)S(1)} %get-tuple-element.370, bf16[512,64]{1,0:T(8,128)(2,1)S(1)} %get-tuple-element.336, bf16[512,64]{1,0:T(8,128)(2,1)S(1)} %get-tuple-element.337), kind=kOutput, calls=%fused_computation.27.clone.1 | convolution fusion | flops 271841280 | bytes 4858368 | tf_op jit(solution)/shard_map/while/body/eval_jaxpr/gqd,gkd->gqk/dot_general | solution.py:36
  57.3 3.6 %fusion.91 = f32[2048]{0:T(1024)S(1)} fusion(f32[512,2048]{1,0:T(8,128)} %get-tuple-element.339, f32[2048]{0:T(1024)S(1)} %bitcast.161, pred[512]{0:T(512)(128)(4,1)S(1)} %broadcast_in_dim.139), kind=kLoop, calls=%fused_computation.28.clone.1 | loop fusion | flops 5240832 | bytes 4211200 | tf_op jit(solution)/shard_map/while/body/eval_jaxpr/reduce_sum | solution.py:43
  60.9 2.0 %fusion.93 = f32[1,2048,128]{2,1,0:T(8,128)S(1)} fusion(bf16[512,128]{1,0:T(8,128)(2,1)S(1)} %bitcast.165, f32[512,2048]{1,0:T(8,128)S(1)} %copy-done, f32[2048]{0:T(1024)S(1)} %bitcast.162, pred[512]{0:T(512)(128)(4,1)S(1)} %broadcast_in_dim.139, f32[1,2048,128]{2,1,0:T(8,128)S(1)} %get-tuple-element.356, f32[2048]{0:T(1024)S(1)} %bitcast.182, ...), kind=kOutput, calls=%fused_computation.31.clone.1 | convolution fusion | flops 274464768 | bytes 6439425 | tf_op jit(solution)/shard_map/while/body/eval_jaxpr/gqk,gkd->gqd/dot_general | solution.py:44
  64.2 1.2 fusion.88
  65.6 2.8 %fusion.89 = (f32[2048]{0:T(1024)S(1)}, f32[512,2048]{1,0:T(8,128)}) fusion(pred[512]{0:T(512)(128)(4,1)S(1)} %broadcast_in_dim.139, bf16[1,2048,128]{2,1,0:T(8,128)(2,1)S(1)} %get-tuple-element.370, bf16[512,64]{1,0:T(8,128)(2,1)S(1)} %get-tuple-element.336, bf16[512,64]{1,0:T(8,128)(2,1)S(1)} %get-tuple-element.337), kind=kOutput, calls=%fused_computation.27.clone.1 | convolution fusion | flops 271841280 | bytes 4858368 | tf_op jit(solution)/shard_map/while/body/eval_jaxpr/gqd,gkd->gqk/dot_general | solution.py:36
  68.4 3.6 %fusion.91 = f32[2048]{0:T(1024)S(1)} fusion(f32[512,2048]{1,0:T(8,128)} %get-tuple-element.339, f32[2048]{0:T(1024)S(1)} %bitcast.161, pred[512]{0:T(512)(128)(4,1)S(1)} %broadcast_in_dim.139), kind=kLoop, calls=%fused_computation.28.clone.1 | loop fusion | flops 5240832 | bytes 4211200 | tf_op jit(solution)/shard_map/while/body/eval_jaxpr/reduce_sum | solution.py:43
  72.0 2.0 %fusion.93 = f32[1,2048,128]{2,1,0:T(8,128)S(1)} fusion(bf16[512,128]{1,0:T(8,128)(2,1)S(1)} %bitcast.165, f32[512,2048]{1,0:T(8,128)S(1)} %copy-done, f32[2048]{0:T(1024)S(1)} %bitcast.162, pred[512]{0:T(512)(128)(4,1)S(1)} %broadcast_in_dim.139, f32[1,2048,128]{2,1,0:T(8,128)S(1)} %get-tuple-element.356, f32[2048]{0:T(1024)S(1)} %bitcast.182, ...), kind=kOutput, calls=%fused_computation.31.clone.1 | convolution fusion | flops 274464768 | bytes 6439425 | tf_op jit(solution)/shard_map/while/body/eval_jaxpr/gqk,gkd->gqd/dot_general | solution.py:44
  75.3 1.2 fusion.88
  76.7 2.8 %fusion.89 = (f32[2048]{0:T(1024)S(1)}, f32[512,2048]{1,0:T(8,128)}) fusion(pred[512]{0:T(512)(128)(4,1)S(1)} %broadcast_in_dim.139, bf16[1,2048,128]{2,1,0:T(8,128)(2,1)S(1)} %get-tuple-element.370, bf16[512,64]{1,0:T(8,128)(2,1)S(1)} %get-tuple-element.336, bf16[512,64]{1,0:T(8,128)(2,1)S(1)} %get-tuple-element.337), kind=kOutput, calls=%fused_computation.27.clone.1 | convolution fusion | flops 271841280 | bytes 4858368 | tf_op jit(solution)/shard_map/while/body/eval_jaxpr/gqd,gkd->gqk/dot_general | solution.py:36
  79.5 3.6 %fusion.91 = f32[2048]{0:T(1024)S(1)} fusion(f32[512,2048]{1,0:T(8,128)} %get-tuple-element.339, f32[2048]{0:T(1024)S(1)} %bitcast.161, pred[512]{0:T(512)(128)(4,1)S(1)} %broadcast_in_dim.139), kind=kLoop, calls=%fused_computation.28.clone.1 | loop fusion | flops 5240832 | bytes 4211200 | tf_op jit(solution)/shard_map/while/body/eval_jaxpr/reduce_sum | solution.py:43
  83.1 2.0 %fusion.93 = f32[1,2048,128]{2,1,0:T(8,128)S(1)} fusion(bf16[512,128]{1,0:T(8,128)(2,1)S(1)} %bitcast.165, f32[512,2048]{1,0:T(8,128)S(1)} %copy-done, f32[2048]{0:T(1024)S(1)} %bitcast.162, pred[512]{0:T(512)(128)(4,1)S(1)} %broadcast_in_dim.139, f32[1,2048,128]{2,1,0:T(8,128)S(1)} %get-tuple-element.356, f32[2048]{0:T(1024)S(1)} %bitcast.182, ...), kind=kOutput, calls=%fused_computation.31.clone.1 | convolution fusion | flops 274464768 | bytes 6439425 | tf_op jit(solution)/shard_map/while/body/eval_jaxpr/gqk,gkd->gqd/dot_general | solution.py:44
  86.4 1.2 fusion.88
  87.8 2.8 %fusion.89 = (f32[2048]{0:T(1024)S(1)}, f32[512,2048]{1,0:T(8,128)}) fusion(pred[512]{0:T(512)(128)(4,1)S(1)} %broadcast_in_dim.139, bf16[1,2048,128]{2,1,0:T(8,128)(2,1)S(1)} %get-tuple-element.370, bf16[512,64]{1,0:T(8,128)(2,1)S(1)} %get-tuple-element.336, bf16[512,64]{1,0:T(8,128)(2,1)S(1)} %get-tuple-element.337), kind=kOutput, calls=%fused_computation.27.clone.1 | convolution fusion | flops 271841280 | bytes 4858368 | tf_op jit(solution)/shard_map/while/body/eval_jaxpr/gqd,gkd->gqk/dot_general | solution.py:36
  90.5 3.6 %fusion.91 = f32[2048]{0:T(1024)S(1)} fusion(f32[512,2048]{1,0:T(8,128)} %get-tuple-element.339, f32[2048]{0:T(1024)S(1)} %bitcast.161, pred[512]{0:T(512)(128)(4,1)S(1)} %broadcast_in_dim.139), kind=kLoop, calls=%fused_computation.28.clone.1 | loop fusion | flops 5240832 | bytes 4211200 | tf_op jit(solution)/shard_map/while/body/eval_jaxpr/reduce_sum | solution.py:43
  94.2 2.0 %fusion.93 = f32[1,2048,128]{2,1,0:T(8,128)S(1)} fusion(bf16[512,128]{1,0:T(8,128)(2,1)S(1)} %bitcast.165, f32[512,2048]{1,0:T(8,128)S(1)} %copy-done, f32[2048]{0:T(1024)S(1)} %bitcast.162, pred[512]{0:T(512)(128)(4,1)S(1)} %broadcast_in_dim.139, f32[1,2048,128]{2,1,0:T(8,128)S(1)} %get-tuple-element.356, f32[2048]{0:T(1024)S(1)} %bitcast.182, ...), kind=kOutput, calls=%fused_computation.31.clone.1 | convolution fusion | flops 274464768 | bytes 6439425 | tf_op jit(solution)/shard_map/while/body/eval_jaxpr/gqk,gkd->gqd/dot_general | solution.py:44
  97.5 1.2 fusion.88
  98.9 2.8 %fusion.89 = (f32[2048]{0:T(1024)S(1)}, f32[512,2048]{1,0:T(8,128)}) fusion(pred[512]{0:T(512)(128)(4,1)S(1)} %broadcast_in_dim.139, bf16[1,2048,128]{2,1,0:T(8,128)(2,1)S(1)} %get-tuple-element.370, bf16[512,64]{1,0:T(8,128)(2,1)S(1)} %get-tuple-element.336, bf16[512,64]{1,0:T(8,128)(2,1)S(1)} %get-tuple-element.337), kind=kOutput, calls=%fused_computation.27.clone.1 | convolution fusion | flops 271841280 | bytes 4858368 | tf_op jit(solution)/shard_map/while/body/eval_jaxpr/gqd,gkd->gqk/dot_general | solution.py:36
  101.6 3.6 %fusion.91 = f32[2048]{0:T(1024)S(1)} fusion(f32[512,2048]{1,0:T(8,128)} %get-tuple-element.339, f32[2048]{0:T(1024)S(1)} %bitcast.161, pred[512]{0:T(512)(128)(4,1)S(1)} %broadcast_in_dim.139), kind=kLoop, calls=%fused_computation.28.clone.1 | loop fusion | flops 5240832 | bytes 4211200 | tf_op jit(solution)/shard_map/while/body/eval_jaxpr/reduce_sum | solution.py:43
  105.3 2.0 %fusion.93 = f32[1,2048,128]{2,1,0:T(8,128)S(1)} fusion(bf16[512,128]{1,0:T(8,128)(2,1)S(1)} %bitcast.165, f32[512,2048]{1,0:T(8,128)S(1)} %copy-done, f32[2048]{0:T(1024)S(1)} %bitcast.162, pred[512]{0:T(512)(128)(4,1)S(1)} %broadcast_in_dim.139, f32[1,2048,128]{2,1,0:T(8,128)S(1)} %get-tuple-element.356, f32[2048]{0:T(1024)S(1)} %bitcast.182, ...), kind=kOutput, calls=%fused_computation.31.clone.1 | convolution fusion | flops 274464768 | bytes 6439425 | tf_op jit(solution)/shard_map/while/body/eval_jaxpr/gqk,gkd->gqd/dot_general | solution.py:44
  108.6 1.2 fusion.88
  110.0 2.8 %fusion.89 = (f32[2048]{0:T(1024)S(1)}, f32[512,2048]{1,0:T(8,128)}) fusion(pred[512]{0:T(512)(128)(4,1)S(1)} %broadcast_in_dim.139, bf16[1,2048,128]{2,1,0:T(8,128)(2,1)S(1)} %get-tuple-element.370, bf16[512,64]{1,0:T(8,128)(2,1)S(1)} %get-tuple-element.336, bf16[512,64]{1,0:T(8,128)(2,1)S(1)} %get-tuple-element.337), kind=kOutput, calls=%fused_computation.27.clone.1 | convolution fusion | flops 271841280 | bytes 4858368 | tf_op jit(solution)/shard_map/while/body/eval_jaxpr/gqd,gkd->gqk/dot_general | solution.py:36
  112.7 3.6 %fusion.91 = f32[2048]{0:T(1024)S(1)} fusion(f32[512,2048]{1,0:T(8,128)} %get-tuple-element.339, f32[2048]{0:T(1024)S(1)} %bitcast.161, pred[512]{0:T(512)(128)(4,1)S(1)} %broadcast_in_dim.139), kind=kLoop, calls=%fused_computation.28.clone.1 | loop fusion | flops 5240832 | bytes 4211200 | tf_op jit(solution)/shard_map/while/body/eval_jaxpr/reduce_sum | solution.py:43
  116.4 2.0 %fusion.93 = f32[1,2048,128]{2,1,0:T(8,128)S(1)} fusion(bf16[512,128]{1,0:T(8,128)(2,1)S(1)} %bitcast.165, f32[512,2048]{1,0:T(8,128)S(1)} %copy-done, f32[2048]{0:T(1024)S(1)} %bitcast.162, pred[512]{0:T(512)(128)(4,1)S(1)} %broadcast_in_dim.139, f32[1,2048,128]{2,1,0:T(8,128)S(1)} %get-tuple-element.356, f32[2048]{0:T(1024)S(1)} %bitcast.182, ...), kind=kOutput, calls=%fused_computation.31.clone.1 | convolution fusion | flops 274464768 | bytes 6439425 | tf_op jit(solution)/shard_map/while/body/eval_jaxpr/gqk,gkd->gqd/dot_general | solution.py:44
  119.6 1.2 fusion.88
  121.0 2.8 %fusion.89 = (f32[2048]{0:T(1024)S(1)}, f32[512,2048]{1,0:T(8,128)}) fusion(pred[512]{0:T(512)(128)(4,1)S(1)} %broadcast_in_dim.139, bf16[1,2048,128]{2,1,0:T(8,128)(2,1)S(1)} %get-tuple-element.370, bf16[512,64]{1,0:T(8,128)(2,1)S(1)} %get-tuple-element.336, bf16[512,64]{1,0:T(8,128)(2,1)S(1)} %get-tuple-element.337), kind=kOutput, calls=%fused_computation.27.clone.1 | convolution fusion | flops 271841280 | bytes 4858368 | tf_op jit(solution)/shard_map/while/body/eval_jaxpr/gqd,gkd->gqk/dot_general | solution.py:36
  123.8 3.6 %fusion.91 = f32[2048]{0:T(1024)S(1)} fusion(f32[512,2048]{1,0:T(8,128)} %get-tuple-element.339, f32[2048]{0:T(1024)S(1)} %bitcast.161, pred[512]{0:T(512)(128)(4,1)S(1)} %broadcast_in_dim.139), kind=kLoop, calls=%fused_computation.28.clone.1 | loop fusion | flops 5240832 | bytes 4211200 | tf_op jit(solution)/shard_map/while/body/eval_jaxpr/reduce_sum | solution.py:43
  127.5 2.0 %fusion.93 = f32[1,2048,128]{2,1,0:T(8,128)S(1)} fusion(bf16[512,128]{1,0:T(8,128)(2,1)S(1)} %bitcast.165, f32[512,2048]{1,0:T(8,128)S(1)} %copy-done, f32[2048]{0:T(1024)S(1)} %bitcast.162, pred[512]{0:T(512)(128)(4,1)S(1)} %broadcast_in_dim.139, f32[1,2048,128]{2,1,0:T(8,128)S(1)} %get-tuple-element.356, f32[2048]{0:T(1024)S(1)} %bitcast.182, ...), kind=kOutput, calls=%fused_computation.31.clone.1 | convolution fusion | flops 274464768 | bytes 6439425 | tf_op jit(solution)/shard_map/while/body/eval_jaxpr/gqk,gkd->gqd/dot_general | solution.py:44
  130.7 1.2 fusion.88
  132.1 2.8 %fusion.89 = (f32[2048]{0:T(1024)S(1)}, f32[512,2048]{1,0:T(8,128)}) fusion(pred[512]{0:T(512)(128)(4,1)S(1)} %broadcast_in_dim.139, bf16[1,2048,128]{2,1,0:T(8,128)(2,1)S(1)} %get-tuple-element.370, bf16[512,64]{1,0:T(8,128)(2,1)S(1)} %get-tuple-element.336, bf16[512,64]{1,0:T(8,128)(2,1)S(1)} %get-tuple-element.337), kind=kOutput, calls=%fused_computation.27.clone.1 | convolution fusion | flops 271841280 | bytes 4858368 | tf_op jit(solution)/shard_map/while/body/eval_jaxpr/gqd,gkd->gqk/dot_general | solution.py:36
  134.9 3.6 %fusion.91 = f32[2048]{0:T(1024)S(1)} fusion(f32[512,2048]{1,0:T(8,128)} %get-tuple-element.339, f32[2048]{0:T(1024)S(1)} %bitcast.161, pred[512]{0:T(512)(128)(4,1)S(1)} %broadcast_in_dim.139), kind=kLoop, calls=%fused_computation.28.clone.1 | loop fusion | flops 5240832 | bytes 4211200 | tf_op jit(solution)/shard_map/while/body/eval_jaxpr/reduce_sum | solution.py:43
  138.5 2.0 %fusion.93 = f32[1,2048,128]{2,1,0:T(8,128)S(1)} fusion(bf16[512,128]{1,0:T(8,128)(2,1)S(1)} %bitcast.165, f32[512,2048]{1,0:T(8,128)S(1)} %copy-done, f32[2048]{0:T(1024)S(1)} %bitcast.162, pred[512]{0:T(512)(128)(4,1)S(1)} %broadcast_in_dim.139, f32[1,2048,128]{2,1,0:T(8,128)S(1)} %get-tuple-element.356, f32[2048]{0:T(1024)S(1)} %bitcast.182, ...), kind=kOutput, calls=%fused_computation.31.clone.1 | convolution fusion | flops 274464768 | bytes 6439425 | tf_op jit(solution)/shard_map/while/body/eval_jaxpr/gqk,gkd->gqd/dot_general | solution.py:44
  140.6 23.9 %while.30 = (s32[]{:T(128)}, f32[1,2048]{1,0:T(1,128)S(1)}, f32[1,2048]{1,0:T(1,128)S(1)}, f32[1,2048,128]{2,1,0:T(8,128)S(1)}, s32[4]{0:T(128)S(1)}, /*index=5*...) while((s32[]{:T(128)}, f32[1,2048]{1,0:T(1,128)S(1)}, ...), condition=%wide.region_9.10_spmd.clone, body=%wide.region_6.9_spmd.clone.sunk | while | flops 554177024 | bytes 16180357 | solution.py:154
  143.7 1.2 fusion.82
  144.9 1.7 fusion.83
  149.7 1.2 fusion.82
  150.9 1.7 fusion.83
  155.6 1.2 fusion.82
  156.9 1.7 fusion.83
  159.8 1.0 dynamic-slice_bitcast_fusion.6
  161.6 1.2 fusion.82
  162.9 1.7 fusion.83
  (199 shorter events, 27.8 us)
Async XLA Ops:
  6.5 21.1 %copy-start.4 = (u32[32]{0:T(128)S(1)}, u32[32]{0:T(128)}, u32[]{:S(2)}) copy-start(u32[32]{0:T(128)} %constant.119) | copy-start | bytes 388
  6.5 22.3 %copy-start.2 = (s32[4]{0:T(128)S(1)}, s32[4]{0:T(128)}, u32[]{:S(2)}) copy-start(s32[4]{0:T(128)} %param.12) | copy-start | bytes 52
  6.5 22.6 %copy-start.3 = (s32[4]{0:T(128)S(1)}, s32[4]{0:T(128)}, u32[]{:S(2)}) copy-start(s32[4]{0:T(128)} %param.13) | copy-start | bytes 52
  6.5 31.1 %copy-start.1 = (bf16[256,1024]{1,0:T(8,128)(2,1)S(1)}, bf16[256,1024]{1,0:T(8,128)(2,1)}, u32[]{:S(2)}) copy-start(bf16[256,1024]{1,0:T(8,128)(2,1)} %param.9) | copy-start | bytes 1572868
  6.5 45.4 %all-gather.3.cloned.1.call-start = ((), (), s32[]{:S(2)}) async-start(), calls=%async_computation.1 | async-start | bytes 2359296 | tf_op jit(solution)/shard_map/all_gather | solution.py:133
  24.7 115.9 %all-gather.5.cloned.1.call-start = ((), (), s32[]{:S(2)}) async-start(), calls=%async_computation.2 | async-start | bytes 1179648 | tf_op jit(solution)/shard_map/all_gather | solution.py:139
  57.3 3.7 %copy-start = (f32[512,2048]{1,0:T(8,128)S(1)}, f32[512,2048]{1,0:T(8,128)}, u32[]{:S(2)}) copy-start(f32[512,2048]{1,0:T(8,128)} %get-tuple-element.339) | copy-start | bytes 12582916 | tf_op jit(solution)/shard_map/while
  68.4 3.7 %copy-start = (f32[512,2048]{1,0:T(8,128)S(1)}, f32[512,2048]{1,0:T(8,128)}, u32[]{:S(2)}) copy-start(f32[512,2048]{1,0:T(8,128)} %get-tuple-element.339) | copy-start | bytes 12582916 | tf_op jit(solution)/shard_map/while
  79.4 3.7 %copy-start = (f32[512,2048]{1,0:T(8,128)S(1)}, f32[512,2048]{1,0:T(8,128)}, u32[]{:S(2)}) copy-start(f32[512,2048]{1,0:T(8,128)} %get-tuple-element.339) | copy-start | bytes 12582916 | tf_op jit(solution)/shard_map/while
  90.5 3.7 %copy-start = (f32[512,2048]{1,0:T(8,128)S(1)}, f32[512,2048]{1,0:T(8,128)}, u32[]{:S(2)}) copy-start(f32[512,2048]{1,0:T(8,128)} %get-tuple-element.339) | copy-start | bytes 12582916 | tf_op jit(solution)/shard_map/while
  101.6 3.7 %copy-start = (f32[512,2048]{1,0:T(8,128)S(1)}, f32[512,2048]{1,0:T(8,128)}, u32[]{:S(2)}) copy-start(f32[512,2048]{1,0:T(8,128)} %get-tuple-element.339) | copy-start | bytes 12582916 | tf_op jit(solution)/shard_map/while
  112.7 3.7 %copy-start = (f32[512,2048]{1,0:T(8,128)S(1)}, f32[512,2048]{1,0:T(8,128)}, u32[]{:S(2)}) copy-start(f32[512,2048]{1,0:T(8,128)} %get-tuple-element.339) | copy-start | bytes 12582916 | tf_op jit(solution)/shard_map/while
  123.8 3.7 %copy-start = (f32[512,2048]{1,0:T(8,128)S(1)}, f32[512,2048]{1,0:T(8,128)}, u32[]{:S(2)}) copy-start(f32[512,2048]{1,0:T(8,128)} %get-tuple-element.339) | copy-start | bytes 12582916 | tf_op jit(solution)/shard_map/while
  134.9 3.7 %copy-start = (f32[512,2048]{1,0:T(8,128)S(1)}, f32[512,2048]{1,0:T(8,128)}, u32[]{:S(2)}) copy-start(f32[512,2048]{1,0:T(8,128)} %get-tuple-element.339) | copy-start | bytes 12582916 | tf_op jit(solution)/shard_map/while
Sparse Core Ops, SparseCore 0:
  24.8 27.0 all-gather.2
  53.8 23.5 all-gather.4
where the time goes:
time: 174 us; the launch traced here: 173 us
  other arithmetic  48.3 us (28%)
  matrix products  47.9 us (28%)
  blocking collectives  23 us (13%)
  local copies, waits for them, and re-layouts  22.8 us (13%)
  between operations  14.2 us (8%)
  waiting for transfers between devices  13 us (7%)
  loops' own time  3.63 us (2%)
    reduce_sum x12, other arithmetic, attend(): totals = totals * factor + jnp.sum(weights, axis=2)  33.5 us
    dot_general x12, matrix products, attend(): jnp.einsum('gqd,gkd->gqk', queries, key_rows, preferred_element_type=jnp....  25 us
    dot_general x12, matrix products, attend(): jnp.einsum('gqk,gkd->gqd', weights.astype(jnp.bfloat16), value_rows, pref...  22.9 us
    all_to_all x1, blocking collectives, shards(): lax.all_to_all(cache_kv, 'pool', split_axis=3, concat_axis=0, tiled=True)  15 us
    all_gather x1, waiting for transfers between devices, shards(): lax.all_gather(local_blocks, 'ctx', axis=0, tiled=True)  12.9 us
    concatenate x10, other arithmetic, rotate(): jnp.concatenate([first_half * cosine - second_half * sine_part, second_ha...  10.5 us
    unnamed x1, blocking collectives  8.02 us
    squeeze x16, local copies, waits for them, and re-layouts, fold_blocks(): lax.scan(fold_advance, carried, (parted, offsets_here, live_here))  7.87 us
  transfers between devices with their start and end apart: 2, of which 1 were waited for; matrix products, arithmetic and copies ran while one was open for 54% of the time, Pallas kernels for 0%

commit v1 on v0

v1 whole, which is shorter than its diff:
```python
import functools
import math

import jax
import jax.numpy as jnp
import numpy as np
from jax import lax
from jax.experimental import pallas as pl
from jax.experimental.pallas import tpu as pltpu
from jax.sharding import PartitionSpec as P

HEAD = 128
HALF = HEAD // 2
ROPE_BASE = 500000.0
MASKED = -1e30
LOG2_SCALE = HEAD**-0.5 * math.log2(math.e)
MESH = pl.DeviceIdType.MESH


def frequency_rows():
    frequency = ROPE_BASE ** (-np.arange(HALF, dtype=np.float64) / HALF)
    return np.tile(np.concatenate([frequency, frequency]).astype(np.float32)[None, :], (8, 1))


def flip_chip(chip, step, chips):
    result, bit = 0, 1
    while bit < chips:
        a = (chip // bit) % 2
        b = (step // bit) % 2
        result = result + bit * (a + b - 2 * a * b)
        bit *= 2
    return result


def signed(sine):
    lane = lax.broadcasted_iota(jnp.int32, sine.shape, 1)
    return jnp.where(lane < HALF, -sine, sine)


def turn(vectors, cosine, sine_signed):
    return vectors * cosine + pltpu.roll(vectors, HALF, 1) * sine_signed


def kernel(
    counts,
    q_hbm,
    kv_hbm,
    cache_hbm,
    place_ref,
    offset_ref,
    freq_ref,
    out_ref,
    q_raw,
    q_rot,
    kv_raw,
    own,
    pas,
    held,
    meta,
    k_now,
    v_now,
    top,
    acc,
    local_sem,
    pool_send,
    pool_recv,
    meta_send,
    meta_recv,
    own_send,
    own_recv,
    own_fwd_send,
    own_fwd_recv,
    pas_send,
    pas_recv,
    pas_fwd_send,
    pas_fwd_recv,
):
    pools, ctxs = counts
    chips = ctxs // 2
    p = lax.axis_index("pool")
    c = lax.axis_index("ctx")
    t = c // 2
    core = c % 2
    sibling = 2 * t + 1 - core
    rows = q_raw.shape[0]
    heads = q_rot.shape[0]
    hold = held.shape[1]
    block = held.shape[3]
    slots = place_ref.shape[0]
    shard = slots * block
    question_start = ctxs * slots * block

    load_q = pltpu.make_async_copy(q_hbm, q_raw, local_sem.at[0])
    load_kv = pltpu.make_async_copy(kv_hbm, kv_raw, local_sem.at[1])
    load_held = pltpu.make_async_copy(
        cache_hbm.at[:, :, :, pl.ds(pl.multiple_of(p * HEAD, HEAD), HEAD)],
        held.at[p],
        local_sem.at[2],
    )
    load_kv.start()
    load_held.start()
    load_q.start()

    barrier = pltpu.get_barrier_semaphore()
    for d in range(1, pools):
        pl.semaphore_signal(barrier, inc=1, device_id=((p + d) % pools, c), device_id_type=MESH)

    def greet(d, _):
        pl.semaphore_signal(barrier, inc=1, device_id=(p, (c + d) % ctxs), device_id_type=MESH)
        return 0

    lax.fori_loop(1, ctxs, greet, 0)

    row8 = lax.broadcasted_iota(jnp.int32, (8, HEAD), 0)
    place_tile = jnp.full((8, HEAD), -1, jnp.int32)
    offset_tile = jnp.zeros((8, HEAD), jnp.int32)
    for i in range(slots):
        place_tile = jnp.where(row8 == i, place_ref[i], place_tile)
        offset_tile = jnp.where(row8 == i, offset_ref[i], offset_tile)
    meta[c, 0] = place_tile
    meta[c, 1] = offset_tile

    freq = freq_ref[0:1, :]
    token = lax.broadcasted_iota(jnp.int32, (rows, HEAD), 0) + (question_start + c * rows)
    angle = token.astype(jnp.float32) * freq
    cos_q = jnp.cos(angle)
    sin_q = signed(jnp.sin(angle))

    load_kv.wait()
    own[c, 0] = turn(kv_raw[0].astype(jnp.float32), cos_q, sin_q).astype(jnp.bfloat16)
    own[c, 1] = kv_raw[1]

    pl.semaphore_wait(barrier, pools - 1 + ctxs - 1)

    def pool_copy(d):
        target = (p + d) % pools
        return pltpu.make_async_remote_copy(
            src_ref=cache_hbm.at[:, :, :, pl.ds(pl.multiple_of(target * HEAD, HEAD), HEAD)],
            dst_ref=held.at[p],
            send_sem=pool_send.at[d],
            recv_sem=pool_recv.at[d],
            device_id=(target, c),
            device_id_type=MESH,
        )

    def meta_copy(d):
        return pltpu.make_async_remote_copy(
            src_ref=meta.at[c],
            dst_ref=meta.at[c],
            send_sem=meta_send.at[d],
            recv_sem=meta_recv.at[d],
            device_id=(p, (c + d) % ctxs),
            device_id_type=MESH,
        )

    def chip_copy(buffer, send, recv, d):
        return pltpu.make_async_remote_copy(
            src_ref=buffer.at[c],
            dst_ref=buffer.at[c],
            send_sem=send.at[d],
            recv_sem=recv.at[d],
            device_id=(p, 2 * flip_chip(t, d, chips) + core),
            device_id_type=MESH,
        )

    def forward_copy(buffer, send, recv, d):
        place = 2 * flip_chip(t, d, chips) + core
        return pltpu.make_async_remote_copy(
            src_ref=buffer.at[place],
            dst_ref=buffer.at[place],
            send_sem=send.at[d],
            recv_sem=recv.at[d],
            device_id=(p, sibling),
            device_id_type=MESH,
        )

    own_sems = (own, own_send, own_recv)
    own_fwd = (own, own_fwd_send, own_fwd_recv)
    pas_sems = (pas, pas_send, pas_recv)
    pas_fwd = (pas, pas_fwd_send, pas_fwd_recv)

    for d in range(1, pools):
        pool_copy(d).start()
    forward_copy(*own_fwd, 0).start()

    def start_meta(d, _):
        meta_copy(d).start()
        return 0

    lax.fori_loop(1, ctxs, start_meta, 0)

    def start_own(d, _):
        @pl.when(flip_chip(t, d, chips) > t)
        def _():
            chip_copy(*own_sems, d).start()

        return 0

    lax.fori_loop(1, chips, start_own, 0)

    load_q.wait()
    for g in range(heads):
        vectors = q_raw[:, g * HEAD : (g + 1) * HEAD].astype(jnp.float32)
        q_rot[g] = turn(vectors, cos_q, sin_q).astype(jnp.bfloat16)

    ones = jnp.ones((2 * shard, HEAD), jnp.bfloat16)

    def attend(keys, first, allowed):
        width = keys.shape[0]
        wide = width // HEAD

        def one_head(g, _):
            scores = lax.dot_general(
                q_rot[g], keys[...], (((1,), (1,)), ((), ())), preferred_element_type=jnp.float32
            )
            if allowed is not None:
                scores = jnp.where(allowed(scores.shape), scores, MASKED)
            peak = jnp.broadcast_to(jnp.max(scores, axis=1, keepdims=True), (rows, HEAD))
            if not first:
                before = top[g]
                peak = jnp.maximum(before, peak)
            weights = jnp.exp2((scores - jnp.concatenate([peak] * wide, axis=1)) * LOG2_SCALE)
            product = jnp.dot(
                weights.astype(jnp.bfloat16), v_now[...], preferred_element_type=jnp.float32
            )
            if first:
                acc[g] = product
            else:
                shrink = jnp.exp2((before - peak) * LOG2_SCALE)
                acc[g] = acc[g] * jnp.concatenate([shrink, shrink], axis=1) + product
            top[g] = peak
            return 0

        lax.fori_loop(0, heads, one_head, 0)

    def gather_chunk(buffer, chip):
        k_now[...] = buffer[pl.ds(2 * chip, 2), 0].reshape(2 * shard, HEAD)
        v_now[:, :HEAD] = buffer[pl.ds(2 * chip, 2), 1].reshape(2 * shard, HEAD)

    forward_copy(*own_fwd, 0).wait_recv()
    gather_chunk(own, t)
    v_now[:, HEAD:] = ones

    def causal(shape):
        key = lax.broadcasted_iota(jnp.int32, shape, 1)
        query = lax.broadcasted_iota(jnp.int32, shape, 0) + core * rows
        return key <= query

    attend(k_now, True, causal)

    def own_step(d, _):
        source = flip_chip(t, d, chips)

        @pl.when(source < t)
        def _():
            chip_copy(*own_sems, d).wait_recv()
            forward_copy(*own_fwd, d).start()
            forward_copy(*own_fwd, d).wait_recv()
            gather_chunk(own, source)
            attend(k_now, False, None)

        return 0

    lax.fori_loop(1, 2, own_step, 0)

    def wait_meta(d, _):
        meta_copy(d).wait_recv()
        return 0

    lax.fori_loop(1, ctxs, wait_meta, 0)
    load_held.wait()
    for d in range(1, pools):
        pool_copy(d).wait_recv()

    places = meta[:, 0]
    offsets = meta[:, 1].astype(jnp.float32)
    live, where_to, rank = [], [], []
    filled = jnp.zeros((1, HEAD), jnp.float32)
    for b in range(pools * hold):
        block_id = ((b // hold) * ctxs + c) * hold + b % hold
        match = jnp.where(places == block_id, 1.0, 0.0)
        live.append(jnp.sum(jnp.sum(match, axis=0), axis=0, keepdims=True))
        where_to.append(jnp.sum(jnp.sum(match * offsets, axis=0), axis=0, keepdims=True))
        rank.append(filled)
        filled = filled + live[-1]
    for k in range(slots):
        key_sum = jnp.zeros((block, HEAD), jnp.float32)
        value_sum = jnp.zeros((block, HEAD), jnp.float32)
        offset = jnp.zeros((1, HEAD), jnp.float32)
        for b in range(pools * hold):
            pick = jnp.where(rank[b] == float(k), live[b], 0.0)
            key_sum = key_sum + pick * held[b // hold, b % hold, 0].astype(jnp.float32)
            value_sum = value_sum + pick * held[b // hold, b % hold, 1].astype(jnp.float32)
            offset = offset + pick * where_to[b]
        angle = jnp.broadcast_to(offset * freq, (8, HEAD))
        cos_k = jnp.cos(angle)[0:1]
        sin_k = signed(jnp.sin(angle))[0:1]
        pas[c, 0, k * block : (k + 1) * block] = turn(key_sum, cos_k, sin_k).astype(jnp.bfloat16)
        pas[c, 1, k * block : (k + 1) * block] = value_sum.astype(jnp.bfloat16)

    forward_copy(*pas_fwd, 0).start()

    def start_pas(d, _):
        chip_copy(*pas_sems, d).start()
        return 0

    lax.fori_loop(1, chips, start_pas, 0)

    lax.fori_loop(2, chips, own_step, 0)

    hold_bits = hold.bit_length() - 1

    def pas_step(d, _):
        source = flip_chip(t, d, chips)

        @pl.when(d > 0)
        def _():
            chip_copy(*pas_sems, d).wait_recv()
            forward_copy(*pas_fwd, d).start()

        forward_copy(*pas_fwd, d).wait_recv()
        v_now[:, :HEAD] = pas[pl.ds(2 * source, 2), 1].reshape(2 * shard, HEAD)
        seen = own[c, 0, 0:16].astype(jnp.float32)[0:1]
        all_places = meta[:, 0]
        holder = lax.shift_right_logical(all_places, hold_bits) & (ctxs - 1)
        for side in range(2):
            column = 2 * source + side
            mine = jnp.where((all_places >= 0) & (holder == column), 1.0, 0.0)
            count = jnp.sum(jnp.sum(mine, axis=0), axis=0, keepdims=True)
            for k in range(slots):
                flag = jnp.broadcast_to(jnp.where(count > float(k), 1.0, 0.0), (block, HEAD))
                at = side * shard + k * block
                keys = pas[column, 0, k * block : (k + 1) * block].astype(jnp.float32)
                k_now[at : at + block] = jnp.where(flag > 0.0, keys, seen).astype(jnp.bfloat16)
                v_now[at : at + block, HEAD:] = flag.astype(jnp.bfloat16)
        attend(k_now, False, None)
        return 0

    lax.fori_loop(0, chips, pas_step, 0)

    for g in range(heads):
        out_ref[:, g * HEAD : (g + 1) * HEAD] = (
            acc[g, :, :HEAD] / acc[g, :, HEAD:]
        ).astype(jnp.bfloat16)

    for d in range(1, pools):
        pool_copy(d).wait_send()

    def end_meta(d, _):
        meta_copy(d).wait_send()
        return 0

    lax.fori_loop(1, ctxs, end_meta, 0)
    forward_copy(*own_fwd, 0).wait_send()
    forward_copy(*pas_fwd, 0).wait_send()

    def end_chips(d, _):
        other = flip_chip(t, d, chips)

        @pl.when(other > t)
        def _():
            chip_copy(*own_sems, d).wait_send()

        @pl.when(other < t)
        def _():
            forward_copy(*own_fwd, d).wait_send()

        chip_copy(*pas_sems, d).wait_send()
        forward_copy(*pas_fwd, d).wait_send()
        return 0

    lax.fori_loop(1, chips, end_chips, 0)


def shards(counts, question_q, question_kv, cache_kv, placement, offsets):
    pools, ctxs = counts
    chips = ctxs // 2
    rows, width = question_q.shape
    heads = width // HEAD
    hold, _, block, _ = cache_kv.shape
    slots = placement.shape[0]
    shard = slots * block
    dma = pltpu.SemaphoreType.DMA
    any_space = pl.BlockSpec(memory_space=pl.ANY)
    return pl.pallas_call(
        functools.partial(kernel, counts),
        out_shape=jax.ShapeDtypeStruct((rows, width), jnp.bfloat16),
        in_specs=[
            any_space,
            any_space,
            any_space,
            pl.BlockSpec(memory_space=pltpu.SMEM),
            pl.BlockSpec(memory_space=pltpu.SMEM),
            pl.BlockSpec(memory_space=pltpu.VMEM),
        ],
        out_specs=pl.BlockSpec(memory_space=pltpu.VMEM),
        scratch_shapes=[
            pltpu.VMEM((rows, width), jnp.bfloat16),
            pltpu.VMEM((heads, rows, HEAD), jnp.bfloat16),
            pltpu.VMEM((2, rows, HEAD), jnp.bfloat16),
            pltpu.VMEM((ctxs, 2, rows, HEAD), jnp.bfloat16),
            pltpu.VMEM((ctxs, 2, shard, HEAD), jnp.bfloat16),
            pltpu.VMEM((pools, hold, 2, block, HEAD), jnp.bfloat16),
            pltpu.VMEM((ctxs, 2, 8, HEAD), jnp.int32),
            pltpu.VMEM((2 * shard, HEAD), jnp.bfloat16),
            pltpu.VMEM((2 * shard, 2 * HEAD), jnp.bfloat16),
            pltpu.VMEM((heads, rows, HEAD), jnp.float32),
            pltpu.VMEM((heads, rows, 2 * HEAD), jnp.float32),
            dma((3,)),
            dma((pools,)),
            dma((pools,)),
            dma((ctxs,)),
            dma((ctxs,)),
            dma((chips,)),
            dma((chips,)),
            dma((chips,)),
            dma((chips,)),
            dma((chips,)),
            dma((chips,)),
            dma((chips,)),
            dma((chips,)),
        ],
        compiler_params=pltpu.CompilerParams(
            collective_id=0, has_side_effects=True, vmem_limit_bytes=40 * 1024 * 1024
        ),
        name="attend_question",
    )(question_q, question_kv, cache_kv, placement, offsets, jnp.asarray(frequency_rows()))


def solution(mesh):
    counts = (mesh.shape["pool"], mesh.shape["ctx"])
    in_specs = (
        P("ctx", "pool"),
        P(None, "ctx", "pool"),
        P(("pool", "ctx"), None, None, None),
        P("ctx"),
        P("ctx"),
    )
    return jax.shard_map(
        functools.partial(shards, counts),
        mesh=mesh,
        in_specs=in_specs,
        out_specs=P("ctx", "pool"),
        check_vma=False,
    )
```

time: 174 us -> 56.1 us (0.32)
  the two profiles are of different devices: /device:TPU:0 before, /device:TPU:7 now
where the time goes in v1:
time: 56.1 us; the launch traced here: 55.9 us
  Pallas kernels  50.2 us (89%)
  local copies, waits for them, and re-layouts  5.69 us (10%)
    pallas_call x1, Pallas kernels, shards(): pl.pallas_call(functools.partial(kernel, counts), out_shape=jax.ShapeDtyp...  50.2 us
    unnamed x13, local copies, waits for them, and re-layouts  5.69 us

profile of v1, /device:TPU:7, one launch (start us, length us, event | category | flops | bytes accessed | tf_op | source)
XLA Modules:
  0.0 55.9 jit_solution(4488162296426698765)
XLA Ops:
  0.0 0.0 copy-start
  0.0 1.0 %copy-done = bf16[256,1024]{1,0:T(8,128)(2,1)S(1)} copy-done((bf16[256,1024]{1,0:T(8,128)(2,1)S(1)}, bf16[256,1024]{1,0:T(8,128)(2,1)}, u32[]{:S(2)}) %copy-start) | copy-done | bytes 524312
  1.0 0.0 copy-start.1
  1.0 0.9 %copy-done.1 = bf16[2,2,64,512]{3,2,1,0:T(8,128)(2,1)S(1)} copy-done((bf16[2,2,64,512]{3,2,1,0:T(8,128)(2,1)S(1)}, bf16[2,2,64,512]{3,2,1,0:T(8,128)(2,1)}, u32[]{:S(2)}) %copy-start.1) | copy-done | bytes 262168
  2.0 0.0 copy-start.2
  2.0 0.9 %copy-done.2 = bf16[2,256,128]{2,1,0:T(8,128)(2,1)S(1)} copy-done((bf16[2,256,128]{2,1,0:T(8,128)(2,1)S(1)}, bf16[2,256,128]{2,1,0:T(8,128)(2,1)}, u32[]{:S(2)}) %copy-start.2) | copy-done | bytes 131096
  2.9 0.0 copy-start.3
  2.9 0.7 %copy-done.3 = f32[8,128]{1,0:T(8,128)S(1)} copy-done((f32[8,128]{1,0:T(8,128)S(1)}, f32[8,128]{1,0:T(8,128)}, u32[]{:S(2)}) %copy-start.3) | copy-done | bytes 4120
  3.6 0.0 copy-start.4
  3.6 0.7 %copy-done.4 = s32[4]{0:T(128)S(1)} copy-done((s32[4]{0:T(128)S(1)}, s32[4]{0:T(128)}, u32[]{:S(2)}) %copy-start.4) | copy-done | bytes 40
  4.2 0.0 copy-start.5
  4.2 0.7 %copy-done.5 = s32[4]{0:T(128)S(1)} copy-done((s32[4]{0:T(128)S(1)}, s32[4]{0:T(128)}, u32[]{:S(2)}) %copy-start.5) | copy-done | bytes 40
  4.9 50.2 %attend_question.1 = bf16[256,1024]{1,0:T(8,128)(2,1)S(1)} custom-call(bf16[256,1024]{1,0:T(8,128)(2,1)S(1)} %copy-done, bf16[2,256,128]{2,1,0:T(8,128)(2,1)S(1)} %copy-done.2, bf16[2,2,64,512]{3,2,1,0:T(8,128)(2,1)S(1)} %copy-done.1, s32[4]{0:T(128)S(1)} %copy-done.4, s32[4]{0:T(128)S(1)} %copy-done.5, f32[8,128]{1,0:T(8,128)S(1)} %copy-done.3), custom_call_target="tpu_custom_call" | custom-call | tf_op jit(solution)/shard_map/attend_question/pallas_call | solution.py:385
  55.1 0.8 %copy.8 = bf16[256,1024]{1,0:T(8,128)(2,1)} copy(bf16[256,1024]{1,0:T(8,128)(2,1)S(1)} %attend_question.1) | data formatting | bytes 1048576
Async XLA Ops:
  0.0 1.0 %copy-start = (bf16[256,1024]{1,0:T(8,128)(2,1)S(1)}, bf16[256,1024]{1,0:T(8,128)(2,1)}, u32[]{:S(2)}) copy-start(bf16[256,1024]{1,0:T(8,128)(2,1)} %q_hbm.1) | copy-start | bytes 1572868
  1.0 0.9 %copy-start.1 = (bf16[2,2,64,512]{3,2,1,0:T(8,128)(2,1)S(1)}, bf16[2,2,64,512]{3,2,1,0:T(8,128)(2,1)}, u32[]{:S(2)}) copy-start(bf16[2,2,64,512]{3,2,1,0:T(8,128)(2,1)} %cache_hbm.1) | copy-start | bytes 786436
  2.0 0.9 %copy-start.2 = (bf16[2,256,128]{2,1,0:T(8,128)(2,1)S(1)}, bf16[2,256,128]{2,1,0:T(8,128)(2,1)}, u32[]{:S(2)}) copy-start(bf16[2,256,128]{2,1,0:T(8,128)(2,1)} %kv_hbm.1) | copy-start | bytes 393220
  2.9 0.7 %copy-start.3 = (f32[8,128]{1,0:T(8,128)S(1)}, f32[8,128]{1,0:T(8,128)}, u32[]{:S(2)}) copy-start(f32[8,128]{1,0:T(8,128)} %constant.2.clone.freq_ref) | copy-start | bytes 12292
  3.6 0.7 %copy-start.4 = (s32[4]{0:T(128)S(1)}, s32[4]{0:T(128)}, u32[]{:S(2)}) copy-start(s32[4]{0:T(128)} %place_ref.1) | copy-start | bytes 52
  4.2 0.7 %copy-start.5 = (s32[4]{0:T(128)S(1)}, s32[4]{0:T(128)}, u32[]{:S(2)}) copy-start(s32[4]{0:T(128)} %offset_ref.1) | copy-start | bytes 52

commit v2 on v1

--- a/solution.py
+++ b/solution.py
@@ -17,9 +17,12 @@
 MESH = pl.DeviceIdType.MESH
 
 
-def frequency_rows():
+def angle_tables(rows):
     frequency = ROPE_BASE ** (-np.arange(HALF, dtype=np.float64) / HALF)
-    return np.tile(np.concatenate([frequency, frequency]).astype(np.float32)[None, :], (8, 1))
+    frequency = np.concatenate([frequency, frequency])
+    angles = np.arange(rows)[:, None] * frequency[None, :]
+    parts = [np.cos(angles), np.sin(angles), np.tile(frequency[None, :], (8, 1))]
+    return np.concatenate(parts).astype(np.float32)
 
 
 def flip_chip(chip, step, chips):
@@ -46,10 +49,13 @@
     q_hbm,
     kv_hbm,
     cache_hbm,
+    place_hbm,
+    offset_hbm,
+    table_hbm,
+    out_ref,
     place_ref,
     offset_ref,
-    freq_ref,
-    out_ref,
+    table_ref,
     q_raw,
     q_rot,
     kv_raw,
@@ -97,7 +103,13 @@
         held.at[p],
         local_sem.at[2],
     )
+    load_table = pltpu.make_async_copy(table_hbm, table_ref, local_sem.at[3])
+    load_place = pltpu.make_async_copy(place_hbm, place_ref, local_sem.at[4])
+    load_offset = pltpu.make_async_copy(offset_hbm, offset_ref, local_sem.at[5])
+    load_place.start()
+    load_offset.start()
     load_kv.start()
+    load_table.start()
     load_held.start()
     load_q.start()
 
@@ -111,6 +123,8 @@
 
     lax.fori_loop(1, ctxs, greet, 0)
 
+    load_place.wait()
+    load_offset.wait()
     row8 = lax.broadcasted_iota(jnp.int32, (8, HEAD), 0)
     place_tile = jnp.full((8, HEAD), -1, jnp.int32)
     offset_tile = jnp.zeros((8, HEAD), jnp.int32)
@@ -120,11 +134,15 @@
     meta[c, 0] = place_tile
     meta[c, 1] = offset_tile
 
-    freq = freq_ref[0:1, :]
-    token = lax.broadcasted_iota(jnp.int32, (rows, HEAD), 0) + (question_start + c * rows)
-    angle = token.astype(jnp.float32) * freq
-    cos_q = jnp.cos(angle)
-    sin_q = signed(jnp.sin(angle))
+    load_table.wait()
+    freq = table_ref[2 * rows : 2 * rows + 8, :]
+    base = (question_start + c * rows).astype(jnp.float32) * freq
+    cos_base = jnp.cos(base)[0:1]
+    sin_base = jnp.sin(base)[0:1]
+    cos_row = table_ref[:rows]
+    sin_row = table_ref[rows : 2 * rows]
+    cos_q = cos_row * cos_base - sin_row * sin_base
+    sin_q = signed(sin_row * cos_base + cos_row * sin_base)
 
     load_kv.wait()
     own[c, 0] = turn(kv_raw[0].astype(jnp.float32), cos_q, sin_q).astype(jnp.bfloat16)
@@ -205,7 +223,7 @@
 
     ones = jnp.ones((2 * shard, HEAD), jnp.bfloat16)
 
-    def attend(keys, first, allowed):
+    def attend(keys, first, allowed, between):
         width = keys.shape[0]
         wide = width // HEAD
 
@@ -231,7 +249,10 @@
             top[g] = peak
             return 0
 
-        lax.fori_loop(0, heads, one_head, 0)
+        half = heads // 2
+        lax.fori_loop(0, half, one_head, 0, unroll=True)
+        between()
+        lax.fori_loop(half, heads, one_head, 0, unroll=True)
 
     def gather_chunk(buffer, chip):
         k_now[...] = buffer[pl.ds(2 * chip, 2), 0].reshape(2 * shard, HEAD)
@@ -246,22 +267,39 @@
         query = lax.broadcasted_iota(jnp.int32, shape, 0) + core * rows
         return key <= query
 
-    attend(k_now, True, causal)
+    def own_arrive(d):
+        @pl.when(flip_chip(t, d, chips) < t)
+        def _():
+            chip_copy(*own_sems, d).wait_recv()
+            forward_copy(*own_fwd, d).start()
+
+    def pas_arrive(d):
+        chip_copy(*pas_sems, d).wait_recv()
+        forward_copy(*pas_fwd, d).start()
+
+    attend(k_now, True, causal, lambda: own_arrive(1))
 
     def own_step(d, _):
         source = flip_chip(t, d, chips)
 
+        def later():
+            @pl.when(d + 1 < chips)
+            def _():
+                own_arrive(d + 1)
+
         @pl.when(source < t)
         def _():
-            chip_copy(*own_sems, d).wait_recv()
-            forward_copy(*own_fwd, d).start()
             forward_copy(*own_fwd, d).wait_recv()
             gather_chunk(own, source)
-            attend(k_now, False, None)
-
-        return 0
-
-    lax.fori_loop(1, 2, own_step, 0)
+            attend(k_now, False, None, later)
+
+        @pl.when(source > t)
+        def _():
+            later()
+
+        return 0
+
+    own_step(1, 0)
 
     def wait_meta(d, _):
         meta_copy(d).wait_recv()
@@ -292,7 +330,7 @@
             key_sum = key_sum + pick * held[b // hold, b % hold, 0].astype(jnp.float32)
             value_sum = value_sum + pick * held[b // hold, b % hold, 1].astype(jnp.float32)
             offset = offset + pick * where_to[b]
-        angle = jnp.broadcast_to(offset * freq, (8, HEAD))
+        angle = offset * freq
         cos_k = jnp.cos(angle)[0:1]
         sin_k = signed(jnp.sin(angle))[0:1]
         pas[c, 0, k * block : (k + 1) * block] = turn(key_sum, cos_k, sin_k).astype(jnp.bfloat16)
@@ -312,11 +350,6 @@
 
     def pas_step(d, _):
         source = flip_chip(t, d, chips)
-
-        @pl.when(d > 0)
-        def _():
-            chip_copy(*pas_sems, d).wait_recv()
-            forward_copy(*pas_fwd, d).start()
 
         forward_copy(*pas_fwd, d).wait_recv()
         v_now[:, :HEAD] = pas[pl.ds(2 * source, 2), 1].reshape(2 * shard, HEAD)
@@ -333,7 +366,13 @@
                 keys = pas[column, 0, k * block : (k + 1) * block].astype(jnp.float32)
                 k_now[at : at + block] = jnp.where(flag > 0.0, keys, seen).astype(jnp.bfloat16)
                 v_now[at : at + block, HEAD:] = flag.astype(jnp.bfloat16)
-        attend(k_now, False, None)
+
+        def later():
+            @pl.when(d + 1 < chips)
+            def _():
+                pas_arrive(d + 1)
+
+        attend(k_now, False, None, later)
         return 0
 
     lax.fori_loop(0, chips, pas_step, 0)
@@ -389,12 +428,15 @@
             any_space,
             any_space,
             any_space,
-            pl.BlockSpec(memory_space=pltpu.SMEM),
-            pl.BlockSpec(memory_space=pltpu.SMEM),
-            pl.BlockSpec(memory_space=pltpu.VMEM),
+            any_space,
+            any_space,
+            any_space,
         ],
         out_specs=pl.BlockSpec(memory_space=pltpu.VMEM),
         scratch_shapes=[
+            pltpu.SMEM((slots,), jnp.int32),
+            pltpu.SMEM((slots,), jnp.int32),
+            pltpu.VMEM((2 * rows + 8, HEAD), jnp.float32),
             pltpu.VMEM((rows, width), jnp.bfloat16),
             pltpu.VMEM((heads, rows, HEAD), jnp.bfloat16),
             pltpu.VMEM((2, rows, HEAD), jnp.bfloat16),
@@ -406,7 +448,7 @@
             pltpu.VMEM((2 * shard, 2 * HEAD), jnp.bfloat16),
             pltpu.VMEM((heads, rows, HEAD), jnp.float32),
             pltpu.VMEM((heads, rows, 2 * HEAD), jnp.float32),
-            dma((3,)),
+            dma((6,)),
             dma((pools,)),
             dma((pools,)),
             dma((ctxs,)),
@@ -421,10 +463,10 @@
             dma((chips,)),
         ],
         compiler_params=pltpu.CompilerParams(
-            collective_id=0, has_side_effects=True, vmem_limit_bytes=40 * 1024 * 1024
+            collective_id=0, has_side_effects=True, vmem_limit_bytes=60 * 1024 * 1024
         ),
         name="attend_question",
-    )(question_q, question_kv, cache_kv, placement, offsets, jnp.asarray(frequency_rows()))
+    )(question_q, question_kv, cache_kv, placement, offsets, jnp.asarray(angle_tables(rows)))
 
 
 def solution(mesh):

time: 56.1 us -> 30.9 us (0.55)
  the two profiles are of different devices: /device:TPU:7 before, /device:TPU:0 now
where the time goes in v2:
time: 30.9 us; the launch traced here: 30.7 us
  Pallas kernels  28.8 us (93%)
  local copies, waits for them, and re-layouts  1.87 us (6%)
    pallas_call x1, Pallas kernels, shards(): pl.pallas_call(functools.partial(kernel, counts), out_shape=jax.ShapeDtyp...  28.8 us
    unnamed x1, local copies, waits for them, and re-layouts  1.87 us

profile of v2, /device:TPU:0, one launch (start us, length us, event | category | flops | bytes accessed | tf_op | source)
XLA Modules:
  0.0 30.7 jit_solution(5277931906915729022)
XLA Ops:
  0.0 28.8 %attend_question.1 = bf16[256,1024]{1,0:T(8,128)(2,1)} custom-call(bf16[256,1024]{1,0:T(8,128)(2,1)} %q_hbm.1, bf16[2,256,128]{2,1,0:T(8,128)(2,1)} %kv_hbm.1, bf16[2,2,64,512]{3,2,1,0:T(8,128)(2,1)} %cache_hbm.1, s32[4]{0:T(128)} %place_hbm.1, s32[4]{0:T(128)} %offset_hbm.1, f32[520,128]{1,0:T(8,128)} %constant.2.clone.table_hbm), custom_call_target="tpu_custom_call" | custom-call | tf_op jit(solution)/shard_map/attend_question/pallas_call | solution.py:424
  28.8 1.9 %copy.8 = bf16[256,1024]{1,0:T(8,128)(2,1)} copy(bf16[256,1024]{1,0:T(8,128)(2,1)} %attend_question.1) | data formatting | bytes 1048576

commit v3 on v2

--- a/solution.py
+++ b/solution.py
@@ -145,7 +145,10 @@
     sin_q = signed(sin_row * cos_base + cos_row * sin_base)
 
     load_kv.wait()
-    own[c, 0] = turn(kv_raw[0].astype(jnp.float32), cos_q, sin_q).astype(jnp.bfloat16)
+    turned = turn(kv_raw[0].astype(jnp.float32), cos_q, sin_q)
+    for j in range(rows // HEAD):
+        tile = turned[j * HEAD : (j + 1) * HEAD]
+        own[c, 0, j * HEAD : (j + 1) * HEAD] = tile.T.astype(jnp.bfloat16)
     own[c, 1] = kv_raw[1]
 
     pl.semaphore_wait(barrier, pools - 1 + ctxs - 1)
@@ -223,50 +226,42 @@
 
     ones = jnp.ones((2 * shard, HEAD), jnp.bfloat16)
 
-    def attend(keys, first, allowed, between):
-        width = keys.shape[0]
+    def attend(first):
+        width = k_now.shape[1]
         wide = width // HEAD
-
-        def one_head(g, _):
-            scores = lax.dot_general(
-                q_rot[g], keys[...], (((1,), (1,)), ((), ())), preferred_element_type=jnp.float32
-            )
-            if allowed is not None:
-                scores = jnp.where(allowed(scores.shape), scores, MASKED)
-            peak = jnp.broadcast_to(jnp.max(scores, axis=1, keepdims=True), (rows, HEAD))
-            if not first:
-                before = top[g]
-                peak = jnp.maximum(before, peak)
-            weights = jnp.exp2((scores - jnp.concatenate([peak] * wide, axis=1)) * LOG2_SCALE)
-            product = jnp.dot(
-                weights.astype(jnp.bfloat16), v_now[...], preferred_element_type=jnp.float32
-            )
-            if first:
-                acc[g] = product
-            else:
-                shrink = jnp.exp2((before - peak) * LOG2_SCALE)
-                acc[g] = acc[g] * jnp.concatenate([shrink, shrink], axis=1) + product
-            top[g] = peak
-            return 0
-
-        half = heads // 2
-        lax.fori_loop(0, half, one_head, 0, unroll=True)
-        between()
-        lax.fori_loop(half, heads, one_head, 0, unroll=True)
+        scores = jnp.dot(
+            q_rot[...].reshape(heads * rows, HEAD), k_now[...], preferred_element_type=jnp.float32
+        )
+        if first:
+            key = lax.broadcasted_iota(jnp.int32, (heads, rows, width), 2)
+            query = lax.broadcasted_iota(jnp.int32, (heads, rows, width), 1) + core * rows
+            scores = jnp.where((key <= query).reshape(scores.shape), scores, MASKED)
+        peak = jnp.broadcast_to(jnp.max(scores, axis=1, keepdims=True), (heads * rows, HEAD))
+        if not first:
+            before = top[...]
+            peak = jnp.maximum(before, peak)
+        weights = jnp.exp2((scores - jnp.concatenate([peak] * wide, axis=1)) * LOG2_SCALE)
+        product = jnp.dot(
+            weights.astype(jnp.bfloat16), v_now[...], preferred_element_type=jnp.float32
+        )
+        if first:
+            acc[...] = product
+        else:
+            shrink = jnp.exp2((before - peak) * LOG2_SCALE)
+            acc[...] = acc[...] * jnp.concatenate([shrink, shrink], axis=1) + product
+        top[...] = peak
 
     def gather_chunk(buffer, chip):
-        k_now[...] = buffer[pl.ds(2 * chip, 2), 0].reshape(2 * shard, HEAD)
+        for side in range(2):
+            for j in range(shard // HEAD):
+                at = side * shard + j * HEAD
+                k_now[:, at : at + HEAD] = buffer[2 * chip + side, 0, j * HEAD : (j + 1) * HEAD]
         v_now[:, :HEAD] = buffer[pl.ds(2 * chip, 2), 1].reshape(2 * shard, HEAD)
 
     forward_copy(*own_fwd, 0).wait_recv()
     gather_chunk(own, t)
     v_now[:, HEAD:] = ones
 
-    def causal(shape):
-        key = lax.broadcasted_iota(jnp.int32, shape, 1)
-        query = lax.broadcasted_iota(jnp.int32, shape, 0) + core * rows
-        return key <= query
-
     def own_arrive(d):
         @pl.when(flip_chip(t, d, chips) < t)
         def _():
@@ -277,7 +272,8 @@
         chip_copy(*pas_sems, d).wait_recv()
         forward_copy(*pas_fwd, d).start()
 
-    attend(k_now, True, causal, lambda: own_arrive(1))
+    own_arrive(1)
+    attend(True)
 
     def own_step(d, _):
         source = flip_chip(t, d, chips)
@@ -291,7 +287,8 @@
         def _():
             forward_copy(*own_fwd, d).wait_recv()
             gather_chunk(own, source)
-            attend(k_now, False, None, later)
+            later()
+            attend(False)
 
         @pl.when(source > t)
         def _():
@@ -321,6 +318,7 @@
         where_to.append(jnp.sum(jnp.sum(match * offsets, axis=0), axis=0, keepdims=True))
         rank.append(filled)
         filled = filled + live[-1]
+    turned_keys = []
     for k in range(slots):
         key_sum = jnp.zeros((block, HEAD), jnp.float32)
         value_sum = jnp.zeros((block, HEAD), jnp.float32)
@@ -333,8 +331,13 @@
         angle = offset * freq
         cos_k = jnp.cos(angle)[0:1]
         sin_k = signed(jnp.sin(angle))[0:1]
-        pas[c, 0, k * block : (k + 1) * block] = turn(key_sum, cos_k, sin_k).astype(jnp.bfloat16)
+        turned_keys.append(turn(key_sum, cos_k, sin_k))
         pas[c, 1, k * block : (k + 1) * block] = value_sum.astype(jnp.bfloat16)
+
+    turned = jnp.concatenate(turned_keys, axis=0)
+    for j in range(shard // HEAD):
+        tile = turned[j * HEAD : (j + 1) * HEAD]
+        pas[c, 0, j * HEAD : (j + 1) * HEAD] = tile.T.astype(jnp.bfloat16)
 
     forward_copy(*pas_fwd, 0).start()
 
@@ -353,7 +356,8 @@
 
         forward_copy(*pas_fwd, d).wait_recv()
         v_now[:, :HEAD] = pas[pl.ds(2 * source, 2), 1].reshape(2 * shard, HEAD)
-        seen = own[c, 0, 0:16].astype(jnp.float32)[0:1]
+        seen = jnp.broadcast_to(own[c, 0, 0:HEAD, 0:1].astype(jnp.float32), (HEAD, HEAD))
+        lane_slot = lax.broadcasted_iota(jnp.int32, (1, HEAD), 1) // block
         all_places = meta[:, 0]
         holder = lax.shift_right_logical(all_places, hold_bits) & (ctxs - 1)
         for side in range(2):
@@ -363,24 +367,31 @@
             for k in range(slots):
                 flag = jnp.broadcast_to(jnp.where(count > float(k), 1.0, 0.0), (block, HEAD))
                 at = side * shard + k * block
-                keys = pas[column, 0, k * block : (k + 1) * block].astype(jnp.float32)
-                k_now[at : at + block] = jnp.where(flag > 0.0, keys, seen).astype(jnp.bfloat16)
                 v_now[at : at + block, HEAD:] = flag.astype(jnp.bfloat16)
+
+            for j in range(shard // HEAD):
+                at = side * shard + j * HEAD
+                slot = (lane_slot + j * (HEAD // block)).astype(jnp.float32)
+                flag = jnp.broadcast_to(jnp.where(count > slot, 1.0, 0.0), (HEAD, HEAD))
+                keys = pas[column, 0, j * HEAD : (j + 1) * HEAD].astype(jnp.float32)
+                k_now[:, at : at + HEAD] = jnp.where(flag > 0.0, keys, seen).astype(jnp.bfloat16)
 
         def later():
             @pl.when(d + 1 < chips)
             def _():
                 pas_arrive(d + 1)
 
-        attend(k_now, False, None, later)
+        later()
+        attend(False)
         return 0
 
     lax.fori_loop(0, chips, pas_step, 0)
 
     for g in range(heads):
-        out_ref[:, g * HEAD : (g + 1) * HEAD] = (
-            acc[g, :, :HEAD] / acc[g, :, HEAD:]
-        ).astype(jnp.bfloat16)
+        part = acc[g * rows : (g + 1) * rows]
+        out_ref[:, g * HEAD : (g + 1) * HEAD] = (part[:, :HEAD] / part[:, HEAD:]).astype(
+            jnp.bfloat16
+        )
 
     for d in range(1, pools):
         pool_copy(d).wait_send()
@@ -420,7 +431,7 @@
     slots = placement.shape[0]
     shard = slots * block
     dma = pltpu.SemaphoreType.DMA
-    any_space = pl.BlockSpec(memory_space=pl.ANY)
+    any_space = pl.BlockSpec(memory_space=pltpu.HBM)
     return pl.pallas_call(
         functools.partial(kernel, counts),
         out_shape=jax.ShapeDtypeStruct((rows, width), jnp.bfloat16),
@@ -444,10 +455,10 @@
             pltpu.VMEM((ctxs, 2, shard, HEAD), jnp.bfloat16),
             pltpu.VMEM((pools, hold, 2, block, HEAD), jnp.bfloat16),
             pltpu.VMEM((ctxs, 2, 8, HEAD), jnp.int32),
-            pltpu.VMEM((2 * shard, HEAD), jnp.bfloat16),
+            pltpu.VMEM((HEAD, 2 * shard), jnp.bfloat16),
             pltpu.VMEM((2 * shard, 2 * HEAD), jnp.bfloat16),
-            pltpu.VMEM((heads, rows, HEAD), jnp.float32),
-            pltpu.VMEM((heads, rows, 2 * HEAD), jnp.float32),
+            pltpu.VMEM((heads * rows, HEAD), jnp.float32),
+            pltpu.VMEM((heads * rows, 2 * HEAD), jnp.float32),
             dma((6,)),
             dma((pools,)),
             dma((pools,)),

time: 30.9 us -> 29.3 us (0.948)
  Pallas kernels: 28.8 us -> 27.2 us
    pallas_call x1, Pallas kernels: 28.8 us -> 27.2 us  [shards(): pl.pallas_call(functools.partial(kernel, counts), out_shape=jax.ShapeDtyp...]
where the time goes in v3:
time: 29.3 us; the launch traced here: 29.1 us
  Pallas kernels  27.2 us (93%)
  local copies, waits for them, and re-layouts  1.87 us (6%)
    pallas_call x1, Pallas kernels, shards(): pl.pallas_call(functools.partial(kernel, counts), out_shape=jax.ShapeDtyp...  27.2 us
    unnamed x1, local copies, waits for them, and re-layouts  1.87 us

profile of v3, /device:TPU:0, one launch (start us, length us, event | category | flops | bytes accessed | tf_op | source)
XLA Modules:
  0.0 29.1 jit_solution(16991881389856732484)
XLA Ops:
  0.0 27.2 %attend_question.1 = bf16[256,1024]{1,0:T(8,128)(2,1)} custom-call(bf16[256,1024]{1,0:T(8,128)(2,1)} %q_hbm.1, bf16[2,256,128]{2,1,0:T(8,128)(2,1)} %kv_hbm.1, bf16[2,2,64,512]{3,2,1,0:T(8,128)(2,1)} %cache_hbm.1, s32[4]{0:T(128)} %place_hbm.1, s32[4]{0:T(128)} %offset_hbm.1, f32[520,128]{1,0:T(8,128)} %constant.2.clone.table_hbm), custom_call_target="tpu_custom_call" | custom-call | tf_op jit(solution)/shard_map/attend_question/pallas_call | solution.py:435
  27.2 1.9 %copy.8 = bf16[256,1024]{1,0:T(8,128)(2,1)} copy(bf16[256,1024]{1,0:T(8,128)(2,1)} %attend_question.1) | data formatting | bytes 1048576

commit v4 on v3

--- a/solution.py
+++ b/solution.py
@@ -272,8 +272,8 @@
         chip_copy(*pas_sems, d).wait_recv()
         forward_copy(*pas_fwd, d).start()
 
+    attend(True)
     own_arrive(1)
-    attend(True)
 
     def own_step(d, _):
         source = flip_chip(t, d, chips)
@@ -295,8 +295,6 @@
             later()
 
         return 0
-
-    own_step(1, 0)
 
     def wait_meta(d, _):
         meta_copy(d).wait_recv()
@@ -347,7 +345,7 @@
 
     lax.fori_loop(1, chips, start_pas, 0)
 
-    lax.fori_loop(2, chips, own_step, 0)
+    lax.fori_loop(1, chips, own_step, 0)
 
     hold_bits = hold.bit_length() - 1
 

time: 29.3 us -> 27 us (0.922)
  Pallas kernels: 27.2 us -> 24.9 us
    pallas_call x1, Pallas kernels: 27.2 us -> 24.9 us  [shards(): pl.pallas_call(functools.partial(kernel, counts), out_shape=jax.ShapeDtyp...]
where the time goes in v4:
time: 27 us; the launch traced here: 26.8 us
  Pallas kernels  24.9 us (92%)
  local copies, waits for them, and re-layouts  1.87 us (7%)
    pallas_call x1, Pallas kernels, shards(): pl.pallas_call(functools.partial(kernel, counts), out_shape=jax.ShapeDtyp...  24.9 us
    unnamed x1, local copies, waits for them, and re-layouts  1.87 us

profile of v4, /device:TPU:0, one launch (start us, length us, event | category | flops | bytes accessed | tf_op | source)
XLA Modules:
  0.0 26.8 jit_solution(3156050237522217315)
XLA Ops:
  0.0 24.9 %attend_question.1 = bf16[256,1024]{1,0:T(8,128)(2,1)} custom-call(bf16[256,1024]{1,0:T(8,128)(2,1)} %q_hbm.1, bf16[2,256,128]{2,1,0:T(8,128)(2,1)} %kv_hbm.1, bf16[2,2,64,512]{3,2,1,0:T(8,128)(2,1)} %cache_hbm.1, s32[4]{0:T(128)} %place_hbm.1, s32[4]{0:T(128)} %offset_hbm.1, f32[520,128]{1,0:T(8,128)} %constant.2.clone.table_hbm), custom_call_target="tpu_custom_call" | custom-call | tf_op jit(solution)/shard_map/attend_question/pallas_call | solution.py:433
  24.9 1.9 %copy.8 = bf16[256,1024]{1,0:T(8,128)(2,1)} copy(bf16[256,1024]{1,0:T(8,128)(2,1)} %attend_question.1) | data formatting | bytes 1048576

commit v5 on v4

--- a/solution.py
+++ b/solution.py
@@ -144,13 +144,6 @@
     cos_q = cos_row * cos_base - sin_row * sin_base
     sin_q = signed(sin_row * cos_base + cos_row * sin_base)
 
-    load_kv.wait()
-    turned = turn(kv_raw[0].astype(jnp.float32), cos_q, sin_q)
-    for j in range(rows // HEAD):
-        tile = turned[j * HEAD : (j + 1) * HEAD]
-        own[c, 0, j * HEAD : (j + 1) * HEAD] = tile.T.astype(jnp.bfloat16)
-    own[c, 1] = kv_raw[1]
-
     pl.semaphore_wait(barrier, pools - 1 + ctxs - 1)
 
     def pool_copy(d):
@@ -202,13 +195,21 @@
 
     for d in range(1, pools):
         pool_copy(d).start()
-    forward_copy(*own_fwd, 0).start()
 
     def start_meta(d, _):
         meta_copy(d).start()
         return 0
 
     lax.fori_loop(1, ctxs, start_meta, 0)
+
+    load_kv.wait()
+    turned = turn(kv_raw[0].astype(jnp.float32), cos_q, sin_q)
+    for j in range(rows // HEAD):
+        tile = turned[j * HEAD : (j + 1) * HEAD]
+        own[c, 0, j * HEAD : (j + 1) * HEAD] = tile.T.astype(jnp.bfloat16)
+    own[c, 1] = kv_raw[1]
+
+    forward_copy(*own_fwd, 0).start()
 
     def start_own(d, _):
         @pl.when(flip_chip(t, d, chips) > t)

time: 27 us -> 26.1 us (0.967)
  the two profiles are of different devices: /device:TPU:0 before, /device:TPU:9 now
where the time goes in v5:
time: 26.1 us; the launch traced here: 25.9 us
  Pallas kernels  24.1 us (92%)
  local copies, waits for them, and re-layouts  1.87 us (7%)
    pallas_call x1, Pallas kernels, shards(): pl.pallas_call(functools.partial(kernel, counts), out_shape=jax.ShapeDtyp...  24.1 us
    unnamed x1, local copies, waits for them, and re-layouts  1.87 us

profile of v5, /device:TPU:9, one launch (start us, length us, event | category | flops | bytes accessed | tf_op | source)
XLA Modules:
  0.0 25.9 jit_solution(8824561672066705540)
XLA Ops:
  0.0 24.1 %attend_question.1 = bf16[256,1024]{1,0:T(8,128)(2,1)} custom-call(bf16[256,1024]{1,0:T(8,128)(2,1)} %q_hbm.1, bf16[2,256,128]{2,1,0:T(8,128)(2,1)} %kv_hbm.1, bf16[2,2,64,512]{3,2,1,0:T(8,128)(2,1)} %cache_hbm.1, s32[4]{0:T(128)} %place_hbm.1, s32[4]{0:T(128)} %offset_hbm.1, f32[520,128]{1,0:T(8,128)} %constant.2.clone.table_hbm), custom_call_target="tpu_custom_call" | custom-call | tf_op jit(solution)/shard_map/attend_question/pallas_call | solution.py:434
  24.1 1.9 %copy.8 = bf16[256,1024]{1,0:T(8,128)(2,1)} copy(bf16[256,1024]{1,0:T(8,128)(2,1)} %attend_question.1) | data formatting | bytes 1048576
